TPU v7x, 32 devices: a whole 2x2x4 slice. The times are simulated.
32 devices in a mesh: dp: 8 (over z, core), expert: 4 (over y, x).
Axes of the slice: x: 2, y: 2, z: 4, core: 2. Of those that a mesh axis runs over, the one named last changes fastest.
Arguments:
- hidden_in: bfloat16 [2048, 2048], P(('dp', 'expert')), parts along dimension 0, may hold values from -6 to 6
- route_ids: int32 [2048, 2], P(('dp', 'expert')), parts along dimension 0, may hold values from 0 to 3, all different within a row; in each aligned block of 64 rows (0 to 63, 64 to 127, ...) at most 64 rows name the same one
- gates: float32 [2048, 2], P(('dp', 'expert')), parts along dimension 0, may hold values from 0.05 to 1
- w_in: bfloat16 [4, 2048, 1536], P('expert'), may hold values from -0.125 to 0.125
- w_out: bfloat16 [4, 768, 2048], P('expert'), may hold values from -0.21875 to 0.21875
Outputs:
- combined: bfloat16 [2048, 2048], P(('dp', 'expert')), parts along dimension 0
There are 8 independent parts, one for each index of `dp`. A program takes and returns all parts, laid end to end along the dimension named above; an argument that names none is the same for every part. Nothing has to cross between parts.
Inputs may be any that keep to these rules, and one draw needn't show every extreme that they name: `route_ids`: each row names 2 different experts. Among the rows of one device (aligned blocks of 64 rows) no expert is named by more than 64 rows, and in every draw some expert is named by exactly 64 rows of some block.
All inputs are finite; a program needn't handle non-finite values.
Results may differ from a plain program's by a relative error of at most 0.0085.
Values may be sent and summed in bfloat16 or wider, within the bound.
A program may use at most 64 MiB of HBM per device.

v0:
```python
import jax
import jax.numpy as jnp
from jax import lax
from jax.sharding import PartitionSpec as P


def slot_ranks(choices, count):
    flat = choices.reshape(choices.shape[:-2] + (-1,))
    length = flat.shape[-1]
    onehot = (flat[..., None] == jnp.arange(count, dtype=jnp.int32)).astype(jnp.bfloat16)
    lower = (
        jnp.arange(length, dtype=jnp.int32)[:, None] > jnp.arange(length, dtype=jnp.int32)[None, :]
    ).astype(jnp.bfloat16)
    ranks = jnp.einsum("ij,...jn->...in", lower, onehot, preferred_element_type=jnp.float32)
    picked = jnp.sum(ranks * onehot.astype(jnp.float32), axis=-1)
    return picked.astype(jnp.int32).reshape(choices.shape)


def body(hidden_in, route_ids, gates, w_in, w_out):
    groups = lax.axis_size("expert")
    rows_here = hidden_in.shape[0]
    capacity = 2 * rows_here * route_ids.shape[1] // groups
    width = hidden_in.shape[1]
    half = w_out.shape[1]
    slots_all = capacity * groups
    slot_of = slot_ranks(route_ids, groups)
    place_key = slot_of * groups + route_ids
    key_table = (place_key[:, :, None] == jnp.arange(slots_all, dtype=jnp.int32)).astype(
        jnp.float32
    )
    placement = jnp.sum(key_table, axis=1).astype(jnp.bfloat16)
    outgoing = jnp.einsum("rs,rd->sd", placement, hidden_in, preferred_element_type=jnp.float32)
    outgoing = outgoing.astype(jnp.bfloat16).reshape(capacity, groups, width)
    projected = jnp.einsum(
        "cnd,df->cnf",
        lax.all_to_all(outgoing, "expert", split_axis=1, concat_axis=1, tiled=True),
        w_in[0],
        preferred_element_type=jnp.float32,
    )
    inner = (jax.nn.silu(projected[..., :half]) * projected[..., half:]).astype(jnp.bfloat16)
    produced = jnp.einsum(
        "cnf,fd->cnd", inner, w_out[0], preferred_element_type=jnp.float32
    ).astype(jnp.bfloat16)
    returned = lax.all_to_all(produced, "expert", split_axis=1, concat_axis=1, tiled=True)
    weighting = jnp.sum(gates[:, :, None] * key_table, axis=1)
    total = jnp.dot(
        weighting,
        returned.reshape(slots_all, width).astype(jnp.float32),
        precision=lax.Precision.HIGHEST,
    )
    return total.astype(jnp.bfloat16)


def solution(mesh):
    placed = (
        P(("dp", "expert"), None),
        P(("dp", "expert"), None),
        P(("dp", "expert"), None),
        P("expert", None, None),
        P("expert", None, None),
    )
    return jax.shard_map(
        body, mesh=mesh, in_specs=placed, out_specs=P(("dp", "expert"), None), check_vma=False
    )
```

profile of v0, /device:TPU:0, one launch (start us, length us, event | category | flops | bytes accessed | tf_op | source)
XLA Modules:
  0.0 56.0 jit_solution(3008103766966193975)
XLA Ops:
  0.0 0.0 copy-start
  0.0 0.9 %copy.20 = s32[64,2]{1,0:T(8,128)S(1)} copy(s32[64,2]{0,1:T(2,128)} %param.6) | data formatting | bytes 1024 | tf_op args[1]
  0.9 0.1 eq.28
  1.1 0.1 fusion.7
  1.2 0.1 mul.30
  1.4 0.1 copy.21
  1.5 0.7 %add.7 = s32[64,2]{0,1:T(2,128)S(1)} add(s32[64,2]{0,1:T(2,128)S(1)} %copy.21, s32[64,2]{0,1:T(2,128)} %param.6) | non-fusion elementwise | flops 128 | bytes 1536 | tf_op jit(solution)/shard_map/add | solution.py:27
  2.2 0.8 %convert_reduce_fusion = (bf16[64,256]{1,0:T(8,128)(2,1)S(1)}, f32[64,256]{1,0:T(8,128)S(1)}) fusion(s32[64,2]{0,1:T(2,128)S(1)} %add.7, f32[64,2]{0,1:T(2,128)} %param.7), kind=kLoop, calls=%fused_computation.12 | loop fusion | flops 131072 | bytes 99328 | tf_op jit(solution)/shard_map/reduce_sum | solution.py:31
  2.9 2.4 %convolution_convert_fusion = bf16[256,2048]{1,0:T(8,128)(2,1)} fusion(bf16[64,2048]{1,0:T(8,128)(2,1)} %param.5, bf16[64,256]{1,0:T(8,128)(2,1)S(1)} %get-tuple-element.5), kind=kOutput, calls=%fused_computation.5 | convolution fusion | flops 67633152 | bytes 1343488 | tf_op jit(solution)/shard_map/rs,rd->sd/dot_general | solution.py:32
  5.3 2.3 %reshape.14 = bf16[64,4,2048]{2,1,0:T(4,128)(2,1)} reshape(bf16[256,2048]{1,0:T(8,128)(2,1)} %convolution_convert_fusion) | data formatting | bytes 2097152 | tf_op jit(solution)/shard_map/reshape | solution.py:33
  7.6 1.8 %copy.22 = bf16[64,4,2048]{2,0,1:T(8,128)(2,1)S(1)} copy(bf16[64,4,2048]{2,1,0:T(4,128)(2,1)} %reshape.14) | data formatting | bytes 2097152 | tf_op jit(solution)/shard_map/reshape | solution.py:33
  9.4 19.1 %all_to_all.10 = bf16[64,4,2048]{2,0,1:T(8,128)(2,1)S(1)} all-to-all(bf16[64,4,2048]{2,0,1:T(8,128)(2,1)S(1)} %copy.22), channel_id=1, replica_groups=mesh['dp'=8,'expert'=4] {'expert'}, dimensions={1} | all-to-all | bytes 2097152 | tf_op jit(solution)/shard_map/all_to_all | solution.py:36
  28.5 4.6 %fusion = f32[64,4,1536]{2,0,1:T(8,128)S(1)} fusion(bf16[64,4,2048]{2,0,1:T(8,128)(2,1)S(1)} %all_to_all.10, bf16[1,2048,1536]{2,1,0:T(8,128)(2,1)} %param.8), kind=kOutput, calls=%fused_computation | convolution fusion | flops 1610612736 | bytes 8912896 | tf_op jit(solution)/shard_map/cnd,df->cnf/dot_general | solution.py:34
  33.1 0.0 copy-done
  33.1 1.0 %fusion.4 = bf16[64,4,2048]{2,0,1:T(8,128)(2,1)S(1)} fusion(bf16[1,768,2048]{2,1,0:T(8,128)(2,1)S(1)} %copy-done, f32[64,4,1536]{2,0,1:T(8,128)S(1)} %fusion), kind=kOutput, calls=%fused_computation.4 | convolution fusion | flops 807010304 | bytes 5767168 | tf_op jit(solution)/shard_map/cnf,fd->cnd/dot_general | solution.py:41
  34.2 15.3 %all_to_all.11 = bf16[64,4,2048]{2,0,1:T(8,128)(2,1)S(1)} all-to-all(bf16[64,4,2048]{2,0,1:T(8,128)(2,1)S(1)} %fusion.4), channel_id=1, replica_groups=mesh['dp'=8,'expert'=4] {'expert'}, dimensions={1} | all-to-all | bytes 2097152 | tf_op jit(solution)/shard_map/all_to_all | solution.py:44
  49.5 1.8 %copy.23 = bf16[64,4,2048]{2,1,0:T(4,128)(2,1)} copy(bf16[64,4,2048]{2,0,1:T(8,128)(2,1)S(1)} %all_to_all.11) | data formatting | bytes 2097152 | tf_op jit(solution)/shard_map/all_to_all | solution.py:44
  51.3 2.2 %reshape.15 = bf16[256,2048]{1,0:T(8,128)(2,1)} reshape(bf16[64,4,2048]{2,1,0:T(4,128)(2,1)} %copy.23) | data formatting | bytes 2097152 | tf_op jit(solution)/shard_map/reshape | solution.py:48
  53.5 2.6 %convolution_convert_fusion.1 = bf16[64,2048]{1,0:T(8,128)(2,1)} fusion(f32[64,256]{1,0:T(8,128)S(1)} %get-tuple-element.6, bf16[256,2048]{1,0:T(8,128)(2,1)} %reshape.15), kind=kOutput, calls=%fused_computation.6 | convolution fusion | flops 402784256 | bytes 1376256 | tf_op jit(solution)/shard_map/dot_general | solution.py:46
  (1 shorter events, 0.0 us)
Async XLA Ops:
  0.0 33.1 %copy-start = (bf16[1,768,2048]{2,1,0:T(8,128)(2,1)S(1)}, bf16[1,768,2048]{2,1,0:T(8,128)(2,1)}, u32[]{:S(2)}) copy-start(bf16[1,768,2048]{2,1,0:T(8,128)(2,1)} %param.9) | copy-start | bytes 9437188
where the time goes:
time: 56.4 us; the launch traced here: 56 us
  blocking collectives  34.4 us (61%)
  matrix products  10.7 us (19%)
  local copies, waits for them, and re-layouts  9.34 us (17%)
  other arithmetic  1.5 us (3%)
    all_to_all x1, blocking collectives, body(): lax.all_to_all(outgoing, 'expert', split_axis=1, concat_axis=1, tiled=True)  19.1 us
    all_to_all x1, blocking collectives, body(): lax.all_to_all(produced, 'expert', split_axis=1, concat_axis=1, tiled=True)  15.3 us
    dot_general x1, matrix products, body(): jnp.einsum('cnd,df->cnf', lax.all_to_all(outgoing, 'expert', split_axis=1...  4.56 us
    reshape x2, local copies, waits for them, and re-layouts, body(): outgoing = outgoing.astype(jnp.bfloat16).reshape(capacity, groups, width)  4.07 us
    dot_general x1, matrix products, body(): jnp.dot(weighting, returned.reshape(slots_all, width).astype(jnp.float32)...  2.58 us
    dot_general x1, matrix products, body(): jnp.einsum('rs,rd->sd', placement, hidden_in, preferred_element_type=jnp....  2.4 us
    reshape x1, local copies, waits for them, and re-layouts, body(): returned.reshape(slots_all, width).astype(jnp.float32)  2.2 us
    all_to_all x1, local copies, waits for them, and re-layouts, body(): lax.all_to_all(produced, 'expert', split_axis=1, concat_axis=1, tiled=True)  1.8 us

commit v1 on v0

--- a/solution.py
+++ b/solution.py
@@ -1,6 +1,8 @@
 import jax
 import jax.numpy as jnp
 from jax import lax
+from jax.experimental import pallas as pl
+from jax.experimental.pallas import tpu as pltpu
 from jax.sharding import PartitionSpec as P
 
 
@@ -50,6 +52,199 @@
     )
     return total.astype(jnp.bfloat16)
 
+CHUNKS = 2
+X, Y, DIAG = 1, 2, 3
+
+
+def quad_kernel(
+    ids_ref, gates_ref, hidden_ref, w_in_ref, w_out_ref, out_ref,
+    win, wout, rows, inner, sums, table, via_x, via_y, fin_x, fin_y,
+    load_sem, table_send, table_recv, go_send, go_recv, back_send, back_recv,
+):
+    me = lax.axis_index("expert")
+    x_bit = lax.rem(me, 2)
+    y_bit = me // 2
+    ids_of = [me, 2 * y_bit + 1 - x_bit, 2 * (1 - y_bit) + x_bit, 3 - me]
+    total_rows, width = hidden_ref.shape
+    step = total_rows // CHUNKS
+    hw = width // 2
+    half = wout.shape[0]
+    left, right = pl.ds(0, hw), pl.ds(hw, hw)
+
+    def remote(src, dst, send, recv, to):
+        return pltpu.make_async_remote_copy(
+            src_ref=src, dst_ref=dst, send_sem=send, recv_sem=recv,
+            device_id={"expert": ids_of[to]}, device_id_type=pl.DeviceIdType.MESH,
+        )
+
+    own = [
+        pltpu.make_async_copy(
+            hidden_ref.at[pl.ds(c * step, step)], rows.at[c, 0], load_sem.at[c]
+        )
+        for c in range(CHUNKS)
+    ]
+    for copy in own:
+        copy.start()
+    load_in = pltpu.make_async_copy(w_in_ref.at[0], win, load_sem.at[CHUNKS])
+    load_out = pltpu.make_async_copy(w_out_ref.at[0], wout, load_sem.at[CHUNKS + 1])
+    load_in.start()
+    load_out.start()
+
+    barrier = pltpu.get_barrier_semaphore()
+    for s in (X, Y, DIAG):
+        pl.semaphore_signal(
+            barrier, inc=1, device_id={"expert": ids_of[s]}, device_id_type=pl.DeviceIdType.MESH
+        )
+
+    for s in range(4):
+        line = jnp.sum(
+            jnp.where(ids_ref[...] == ids_of[s], gates_ref[...], jnp.float32(0.0)),
+            axis=0, keepdims=True,
+        )
+        tile = 0 if s == 0 else 3 + s
+        table[tile] = jnp.zeros_like(table[tile])
+        table[tile, :, :total_rows] = jnp.broadcast_to(line, (8, total_rows))
+    pl.semaphore_wait(barrier, 3)
+
+    def go(c, index, src, dst_slot, cols, to):
+        return remote(
+            src, rows.at[c, dst_slot, :, cols], go_send.at[c, index], go_recv.at[c, index], to
+        )
+
+    sent = []
+    for c in range(CHUNKS):
+        own[c].wait()
+        for index, cols, to in ((0, left, X), (1, right, Y), (2, right, X), (3, left, Y)):
+            copy = go(c, index, rows.at[c, 0, :, cols], to, cols, to)
+            copy.start()
+            sent.append(copy)
+        if c == 0:
+            tables = [
+                remote(table.at[3 + s], table.at[s], table_send.at[s - 1], table_recv.at[s - 1], s)
+                for s in (X, Y, DIAG)
+            ]
+            for copy in tables:
+                copy.start()
+
+    def forward(c):
+        first, second = sent[4 * c], sent[4 * c + 1]
+        on_y = go(c, 4, rows.at[c, X, :, left], DIAG, left, Y)
+        on_x = go(c, 5, rows.at[c, Y, :, right], DIAG, right, X)
+        first.wait_recv()
+        on_y.start()
+        second.wait_recv()
+        on_x.start()
+        return on_y, on_x
+
+    forwards = [forward(0)]
+    columns = None
+    back = []
+    for c in range(CHUNKS):
+        if c + 1 < CHUNKS:
+            forwards.append(forward(c + 1))
+        sent[4 * c + 2].wait_recv()
+        sent[4 * c + 3].wait_recv()
+        if c == 0:
+            for copy in tables:
+                copy.wait_recv()
+            columns = [jnp.transpose(table[s])[:total_rows, 0:1] for s in range(4)]
+            load_in.wait()
+        for copy in forwards[c]:
+            copy.wait_recv()
+        x = rows[c].reshape(4 * step, width)
+        for f in range(0, half, 256):
+            gate = jnp.dot(x, win[:, f : f + 256], preferred_element_type=jnp.float32)
+            up = jnp.dot(
+                x, win[:, half + f : half + f + 256], preferred_element_type=jnp.float32
+            )
+            inner[:, f : f + 256] = (gate / (1.0 + jnp.exp(-gate)) * up).astype(inner.dtype)
+        if c == 0:
+            load_out.wait()
+        h = inner[...]
+        weight = jnp.concatenate([col[c * step : (c + 1) * step] for col in columns], axis=0)
+        for d in range(0, width, 512):
+            made = jnp.dot(h, wout[:, d : d + 512], preferred_element_type=jnp.float32)
+            sums[c, :, :, d : d + 512] = (
+                (made * weight).astype(sums.dtype).reshape(4, step, 512)
+            )
+
+        def send(index, src, dst, to):
+            copy = remote(src, dst, back_send.at[c, index], back_recv.at[c, index], to)
+            copy.start()
+            return copy
+
+        back.append([
+            send(0, sums.at[c, DIAG, :, left], via_x.at[c], X),
+            send(1, sums.at[c, DIAG, :, right], via_y.at[c], Y),
+            send(2, sums.at[c, X, :, left], fin_x.at[c, :, left], X),
+            send(3, sums.at[c, Y, :, right], fin_y.at[c, :, right], Y),
+        ])
+
+    for c in range(CHUNKS):
+        def relay(index, came, slot, cols, held, dst):
+            came.wait_recv()
+            sums[c, slot, :, cols] = (
+                sums[c, slot, :, cols].astype(jnp.float32) + held[c].astype(jnp.float32)
+            ).astype(sums.dtype)
+            copy = remote(
+                sums.at[c, slot, :, cols], dst, back_send.at[c, index], back_recv.at[c, index], slot
+            )
+            copy.start()
+            return copy
+
+        back[c].append(relay(4, back[c][0], Y, left, via_x, fin_y.at[c, :, left]))
+        back[c].append(relay(5, back[c][1], X, right, via_y, fin_x.at[c, :, right]))
+
+    for c in range(CHUNKS):
+        for copy in back[c][2:]:
+            copy.wait_recv()
+        out_ref[pl.ds(c * step, step), :] = (
+            sums[c, 0].astype(jnp.float32)
+            + fin_x[c].astype(jnp.float32)
+            + fin_y[c].astype(jnp.float32)
+        ).astype(out_ref.dtype)
+
+    for copy in sent + tables + [f for pair in forwards for f in pair] + sum(back, []):
+        copy.wait_send()
+
+
+def quad_body(hidden_in, route_ids, gates, w_in, w_out):
+    rows, width = hidden_in.shape
+    half = w_out.shape[1]
+    step = rows // CHUNKS
+    kind = hidden_in.dtype
+    vmem = pl.BlockSpec(memory_space=pltpu.VMEM)
+    anywhere = pl.BlockSpec(memory_space=pl.ANY)
+    dma = pltpu.SemaphoreType.DMA
+    return pl.pallas_call(
+        quad_kernel,
+        out_shape=jax.ShapeDtypeStruct((rows, width), kind),
+        in_specs=[vmem, vmem, anywhere, anywhere, anywhere],
+        out_specs=vmem,
+        scratch_shapes=[
+            pltpu.VMEM((width, 2 * half), kind),
+            pltpu.VMEM((half, width), kind),
+            pltpu.VMEM((CHUNKS, 4, step, width), kind),
+            pltpu.VMEM((4 * step, half), kind),
+            pltpu.VMEM((CHUNKS, 4, step, width), kind),
+            pltpu.VMEM((7, 8, 128), jnp.float32),
+            pltpu.VMEM((CHUNKS, step, width // 2), kind),
+            pltpu.VMEM((CHUNKS, step, width // 2), kind),
+            pltpu.VMEM((CHUNKS, step, width), kind),
+            pltpu.VMEM((CHUNKS, step, width), kind),
+            dma((CHUNKS + 2,)),
+            dma((3,)),
+            dma((3,)),
+            dma((CHUNKS, 6)),
+            dma((CHUNKS, 6)),
+            dma((CHUNKS, 6)),
+            dma((CHUNKS, 6)),
+        ],
+        compiler_params=pltpu.CompilerParams(
+            collective_id=0, has_side_effects=True, vmem_limit_bytes=56 * 1024 * 1024
+        ),
+    )(route_ids.T, gates.T, hidden_in, w_in, w_out)
+
 
 def solution(mesh):
     placed = (
@@ -59,6 +254,7 @@
         P("expert", None, None),
         P("expert", None, None),
     )
+    local = quad_body if mesh.shape["expert"] == 4 else body
     return jax.shard_map(
-        body, mesh=mesh, in_specs=placed, out_specs=P(("dp", "expert"), None), check_vma=False
-    )
+        local, mesh=mesh, in_specs=placed, out_specs=P(("dp", "expert"), None), check_vma=False
+    )

time: 56.4 us -> 28 us (0.50)
  blocking collectives: 34.4 us -> 0 us
  Pallas kernels: 0 us -> 26.2 us
  matrix products: 10.7 us -> 0 us
  local copies, waits for them, and re-layouts: 9.34 us -> 1.67 us
  other arithmetic: 1.5 us -> 0 us
    all_to_all x2 -> x0, blocking collectives: 34.4 us -> none  [the longest x1 19.1 us: body(): lax.all_to_all(outgoing, 'expert', split_axis=1, concat_axis=1, tiled=True)]
    pallas_call x0 -> x1, Pallas kernels: none -> 26.2 us  [quad_body(): pl.pallas_call(quad_kernel, out_shape=jax.ShapeDtypeStruct((rows, width),...]
    dot_general x5 -> x0, matrix products: 10.7 us -> none  [the longest x1 4.56 us: body(): jnp.einsum('cnd,df->cnf', lax.all_to_all(outgoing, 'expert', split_axis=1...]
    reshape x3 -> x0, local copies, waits for them, and re-layouts: 6.27 us -> none  [the longest x2 4.07 us: body(): outgoing = outgoing.astype(jnp.bfloat16).reshape(capacity, groups, width)]
    all_to_all x1 -> x0, local copies, waits for them, and re-layouts: 1.8 us -> none  [body(): lax.all_to_all(produced, 'expert', split_axis=1, concat_axis=1, tiled=True)]
    reduce_sum x1 -> x0, other arithmetic: 0.78 us -> none  [body(): placement = jnp.sum(key_table, axis=1).astype(jnp.bfloat16)]
    unnamed x3 -> x1, local copies, waits for them, and re-layouts: 0.92 us -> 1.67 us
    add x1 -> x0, other arithmetic: 0.7 us -> none  [body(): place_key = slot_of * groups + route_ids]
where the time goes in v1:
time: 28 us; the launch traced here: 27.9 us
  Pallas kernels  26.2 us (94%)
  local copies, waits for them, and re-layouts  1.67 us (6%)
    pallas_call x1, Pallas kernels, quad_body(): pl.pallas_call(quad_kernel, out_shape=jax.ShapeDtypeStruct((rows, width),...  26.2 us
    unnamed x1, local copies, waits for them, and re-layouts  1.67 us

profile of v1, /device:TPU:0, one launch (start us, length us, event | category | flops | bytes accessed | tf_op | source)
XLA Modules:
  0.0 27.9 jit_solution(8131193452477874358)
XLA Ops:
  0.0 26.2 %shard_map.55 = bf16[64,2048]{1,0:T(8,128)(2,1)} custom-call(s32[2,64]{1,0:T(2,128)} %bitcast.2, f32[2,64]{1,0:T(2,128)} %bitcast.3, bf16[64,2048]{1,0:T(8,128)(2,1)} %hidden_ref.1, bf16[1,2048,1536]{2,1,0:T(8,128)(2,1)} %w_in_ref.1, bf16[1,768,2048]{2,1,0:T(8,128)(2,1)} %w_out_ref.1), custom_call_target="tpu_custom_call" | custom-call | tf_op jit(solution)/shard_map/pallas_call | solution.py:219
  26.2 1.7 %copy.7 = bf16[64,2048]{1,0:T(8,128)(2,1)} copy(bf16[64,2048]{1,0:T(8,128)(2,1)} %shard_map.55) | data formatting | bytes 524288

commit v2 on v1

--- a/solution.py
+++ b/solution.py
@@ -67,9 +67,9 @@
     ids_of = [me, 2 * y_bit + 1 - x_bit, 2 * (1 - y_bit) + x_bit, 3 - me]
     total_rows, width = hidden_ref.shape
     step = total_rows // CHUNKS
-    hw = width // 2
+    part = step // 2
     half = wout.shape[0]
-    left, right = pl.ds(0, hw), pl.ds(hw, hw)
+    low, high = pl.ds(0, part), pl.ds(part, part)
 
     def remote(src, dst, send, recv, to):
         return pltpu.make_async_remote_copy(
@@ -106,44 +106,45 @@
         table[tile, :, :total_rows] = jnp.broadcast_to(line, (8, total_rows))
     pl.semaphore_wait(barrier, 3)
 
-    def go(c, index, src, dst_slot, cols, to):
-        return remote(
-            src, rows.at[c, dst_slot, :, cols], go_send.at[c, index], go_recv.at[c, index], to
-        )
-
-    sent = []
-    for c in range(CHUNKS):
+    def go(c, index, src_slot, dst_slot, span, to):
+        copy = remote(
+            rows.at[c, src_slot, span], rows.at[c, dst_slot, span],
+            go_send.at[c, index], go_recv.at[c, index], to,
+        )
+        copy.start()
+        return copy
+
+    def first_half(c):
         own[c].wait()
-        for index, cols, to in ((0, left, X), (1, right, Y), (2, right, X), (3, left, Y)):
-            copy = go(c, index, rows.at[c, 0, :, cols], to, cols, to)
-            copy.start()
-            sent.append(copy)
-        if c == 0:
-            tables = [
-                remote(table.at[3 + s], table.at[s], table_send.at[s - 1], table_recv.at[s - 1], s)
-                for s in (X, Y, DIAG)
-            ]
-            for copy in tables:
-                copy.start()
-
-    def forward(c):
-        first, second = sent[4 * c], sent[4 * c + 1]
-        on_y = go(c, 4, rows.at[c, X, :, left], DIAG, left, Y)
-        on_x = go(c, 5, rows.at[c, Y, :, right], DIAG, right, X)
-        first.wait_recv()
-        on_y.start()
-        second.wait_recv()
-        on_x.start()
-        return on_y, on_x
-
-    forwards = [forward(0)]
+        return [go(c, 0, 0, X, low, X), go(c, 1, 0, Y, high, Y)]
+
+    def second_half(c):
+        return [go(c, 2, 0, X, high, X), go(c, 3, 0, Y, low, Y)]
+
+    def forward(first):
+        c, (from_x, from_y) = first
+        from_x.wait_recv()
+        on_y = go(c, 4, X, DIAG, low, Y)
+        from_y.wait_recv()
+        return [on_y, go(c, 5, Y, DIAG, high, X)]
+
+    firsts, seconds, forwards = [first_half(0)], [second_half(0)], []
+    tables = [
+        remote(table.at[3 + s], table.at[s], table_send.at[s - 1], table_recv.at[s - 1], s)
+        for s in (X, Y, DIAG)
+    ]
+    for copy in tables:
+        copy.start()
+    for c in range(1, CHUNKS):
+        firsts.append(first_half(c))
+        forwards.append(forward((c - 1, firsts[c - 1])))
+        seconds.append(second_half(c))
+    forwards.append(forward((CHUNKS - 1, firsts[-1])))
     columns = None
     back = []
     for c in range(CHUNKS):
-        if c + 1 < CHUNKS:
-            forwards.append(forward(c + 1))
-        sent[4 * c + 2].wait_recv()
-        sent[4 * c + 3].wait_recv()
+        for copy in seconds[c]:
+            copy.wait_recv()
         if c == 0:
             for copy in tables:
                 copy.wait_recv()
@@ -174,26 +175,26 @@
             return copy
 
         back.append([
-            send(0, sums.at[c, DIAG, :, left], via_x.at[c], X),
-            send(1, sums.at[c, DIAG, :, right], via_y.at[c], Y),
-            send(2, sums.at[c, X, :, left], fin_x.at[c, :, left], X),
-            send(3, sums.at[c, Y, :, right], fin_y.at[c, :, right], Y),
+            send(0, sums.at[c, DIAG, low], via_x.at[c], X),
+            send(1, sums.at[c, DIAG, high], via_y.at[c], Y),
+            send(2, sums.at[c, X, low], fin_x.at[c, low], X),
+            send(3, sums.at[c, Y, high], fin_y.at[c, high], Y),
         ])
 
     for c in range(CHUNKS):
-        def relay(index, came, slot, cols, held, dst):
+        def relay(index, came, slot, span, held, dst):
             came.wait_recv()
-            sums[c, slot, :, cols] = (
-                sums[c, slot, :, cols].astype(jnp.float32) + held[c].astype(jnp.float32)
+            sums[c, slot, span] = (
+                sums[c, slot, span].astype(jnp.float32) + held[c].astype(jnp.float32)
             ).astype(sums.dtype)
             copy = remote(
-                sums.at[c, slot, :, cols], dst, back_send.at[c, index], back_recv.at[c, index], slot
+                sums.at[c, slot, span], dst, back_send.at[c, index], back_recv.at[c, index], slot
             )
             copy.start()
             return copy
 
-        back[c].append(relay(4, back[c][0], Y, left, via_x, fin_y.at[c, :, left]))
-        back[c].append(relay(5, back[c][1], X, right, via_y, fin_x.at[c, :, right]))
+        back[c].append(relay(4, back[c][0], Y, low, via_x, fin_y.at[c, low]))
+        back[c].append(relay(5, back[c][1], X, high, via_y, fin_x.at[c, high]))
 
     for c in range(CHUNKS):
         for copy in back[c][2:]:
@@ -204,7 +205,7 @@
             + fin_y[c].astype(jnp.float32)
         ).astype(out_ref.dtype)
 
-    for copy in sent + tables + [f for pair in forwards for f in pair] + sum(back, []):
+    for copy in tables + sum(firsts + seconds + forwards + back, []):
         copy.wait_send()
 
 
@@ -218,7 +219,7 @@
     dma = pltpu.SemaphoreType.DMA
     return pl.pallas_call(
         quad_kernel,
-        out_shape=jax.ShapeDtypeStruct((rows, width), kind),
+        out_shape=pltpu.VMEM((rows, width), kind),
         in_specs=[vmem, vmem, anywhere, anywhere, anywhere],
         out_specs=vmem,
         scratch_shapes=[
@@ -228,8 +229,8 @@
             pltpu.VMEM((4 * step, half), kind),
             pltpu.VMEM((CHUNKS, 4, step, width), kind),
             pltpu.VMEM((7, 8, 128), jnp.float32),
-            pltpu.VMEM((CHUNKS, step, width // 2), kind),
-            pltpu.VMEM((CHUNKS, step, width // 2), kind),
+            pltpu.VMEM((CHUNKS, step // 2, width), kind),
+            pltpu.VMEM((CHUNKS, step // 2, width), kind),
             pltpu.VMEM((CHUNKS, step, width), kind),
             pltpu.VMEM((CHUNKS, step, width), kind),
             dma((CHUNKS + 2,)),

time: 28 us -> 25.7 us (0.918)
  Pallas kernels: 26.2 us -> 24.8 us
  local copies, waits for them, and re-layouts: 1.67 us -> 0.71 us
    pallas_call x1, Pallas kernels: 26.2 us -> 24.8 us  [quad_body(): pl.pallas_call(quad_kernel, out_shape=pltpu.VMEM((rows, width), kind), in...]
    unnamed x1, local copies, waits for them, and re-layouts: 1.67 us -> 0.71 us
where the time goes in v2:
time: 25.7 us; the launch traced here: 25.6 us
  Pallas kernels  24.8 us (96%)
  local copies, waits for them, and re-layouts  0.71 us (3%)
    pallas_call x1, Pallas kernels, quad_body(): pl.pallas_call(quad_kernel, out_shape=pltpu.VMEM((rows, width), kind), in...  24.8 us
    unnamed x1, local copies, waits for them, and re-layouts  0.71 us

profile of v2, /device:TPU:0, one launch (start us, length us, event | category | flops | bytes accessed | tf_op | source)
XLA Modules:
  0.0 25.6 jit_solution(11033715075132387819)
XLA Ops:
  0.0 24.8 %shard_map.55 = bf16[64,2048]{1,0:T(8,128)(2,1)S(1)} custom-call(s32[2,64]{1,0:T(2,128)} %bitcast.2, f32[2,64]{1,0:T(2,128)} %bitcast.3, bf16[64,2048]{1,0:T(8,128)(2,1)} %hidden_ref.1, bf16[1,2048,1536]{2,1,0:T(8,128)(2,1)} %w_in_ref.1, bf16[1,768,2048]{2,1,0:T(8,128)(2,1)} %w_out_ref.1), custom_call_target="tpu_custom_call" | custom-call | tf_op jit(solution)/shard_map/pallas_call | solution.py:220
  24.9 0.7 %copy.7 = bf16[64,2048]{1,0:T(8,128)(2,1)} copy(bf16[64,2048]{1,0:T(8,128)(2,1)S(1)} %shard_map.55) | data formatting | bytes 524288
